TPU v7x, 32 devices: a whole 2x2x4 slice. The times are simulated.
32 devices in a mesh: grp: 4 (over z), wide: 8 (over y, x, core).
Axes of the slice: x: 2, y: 2, z: 4, core: 2. Of those that a mesh axis runs over, the one named last changes fastest.
Arguments:
- visibilities: bfloat16 [2, 8, 2048, 4096], P(None, None, 'wide', 'grp'), may hold values from -6 to 6
- filters: bfloat16 [4096, 64, 2048], P(('grp', 'wide')), may hold values from -0.125 to 0.125
- counts: int32 [4096], replicated, may hold values from 128 to 2048, as said below
- m_of_slot: int32 [4096], replicated, may hold values from 0 to 4095, each once
- band_of_block: int32 [4096, 8], replicated, may hold values from 0 to 1023
Outputs:
- kl_coeffs: bfloat16 [4096, 2, 8, 64], P(('grp', 'wide'))
- band_power: float32 [8, 1024], P(None, ('grp', 'wide'))
Inputs may be any that keep to these rules, and one draw needn't show every extreme that they name: Mode m uses its first counts[m] baselines; both ends of the range are taken in every draw. `m_of_slot`: each m mode stands in exactly one slot.
All inputs are finite; a program needn't handle non-finite values.
Results may differ from a plain program's by a relative error of at most 0.0055.
Values may be sent and summed in bfloat16 or wider, within the bound.
A program may use at most 128 MiB of HBM per device.

v0:
```python
import math

import jax
import jax.numpy as jnp
from jax import lax
from jax.sharding import PartitionSpec as P

NB = 2048
NT = 4096
KL = 64
KB = 8
NBAND = 1024
NKB = 8


def table_block(columns):
    times = jnp.arange(NT, dtype=jnp.int32)
    index = times[:, None] * columns[None, :] % NT
    angles = index.astype(jnp.float32) * (2.0 * math.pi / NT)
    return (jnp.cos(angles).astype(jnp.bfloat16), jnp.sin(angles).astype(jnp.bfloat16))


def body(visibilities, filters, counts, m_of_slot, band_of_block):
    highest = lax.Precision.HIGHEST
    channels = visibilities.shape[1]
    local = lax.all_to_all(visibilities, "grp", split_axis=2, concat_axis=3, tiled=True)
    base_dev = local.shape[2]
    rows = channels * base_dev
    real_part = local[0].reshape(rows, NT)
    imag_part = local[1].reshape(rows, NT)
    scale_dft = 1.0 / math.sqrt(NT)
    mode_block = min(512, NT)

    def product(table, values):
        return jnp.einsum("tm,rt->mr", table, values, preferred_element_type=jnp.float32)

    def transform(columns):
        cos_table, sin_table = table_block(columns)
        spec_re = (product(cos_table, real_part) + product(sin_table, imag_part)) * scale_dft
        spec_im = (product(cos_table, imag_part) - product(sin_table, real_part)) * scale_dft
        return jnp.stack([spec_re, spec_im]).astype(jnp.bfloat16)

    blocks = lax.map(transform, m_of_slot.reshape(NT // mode_block, mode_block))
    spectrum = blocks.transpose(1, 0, 2, 3).reshape(2, NT, rows)
    groups = lax.axis_size("grp")
    wides = lax.axis_size("wide")
    slots = NT // (groups * wides)
    moved = lax.all_to_all(spectrum, ("grp", "wide"), split_axis=1, concat_axis=2, tiled=True)
    owned = moved.reshape(2, slots, groups, wides, channels, base_dev).transpose(1, 0, 4, 3, 2, 5)
    owned = owned.reshape(slots, 2, channels, NB)
    place = lax.axis_index(("grp", "wide"))
    mine = lax.dynamic_slice_in_dim(m_of_slot, place * slots, slots)
    active_counts = counts[mine]
    band_rows = band_of_block[mine]
    active = jnp.arange(NB, dtype=jnp.int32)[None, :] < active_counts[:, None]
    masked = jnp.where(active[:, None, None, :], owned, jnp.zeros_like(owned))
    coeffs = jnp.einsum("sxcb,skb->sxck", masked, filters, preferred_element_type=jnp.float32)
    kl_coeffs = coeffs.astype(jnp.bfloat16)
    power = coeffs[:, 0] * coeffs[:, 0] + coeffs[:, 1] * coeffs[:, 1]
    block_power = power.reshape(slots, channels, NKB, KB).sum(axis=-1)
    one_hot = (band_rows[:, :, None] == jnp.arange(NBAND, dtype=jnp.int32)[None, None, :]).astype(
        jnp.float32
    )
    partial_sums = jnp.einsum("scj,sjn->cn", block_power, one_hot, precision=highest)
    band_scale = NBAND / (NT * KL)
    totals = lax.psum(partial_sums, ("grp", "wide"))
    band_dev = NBAND // (groups * wides)
    band_power = lax.dynamic_slice_in_dim(totals, place * band_dev, band_dev, 1) * band_scale
    return (kl_coeffs, band_power)


def solution(mesh):
    placed = (P(None, None, "wide", "grp"), P(("grp", "wide"), None, None), P(), P(), P())
    return jax.shard_map(
        body,
        mesh=mesh,
        in_specs=placed,
        out_specs=(P(("grp", "wide"), None, None, None), P(None, ("grp", "wide"))),
        check_vma=False,
    )
```

profile of v0, /device:TPU:0, one launch (start us, length us, event | category | flops | bytes accessed | tf_op | source)
XLA Modules:
  0.0 1608.5 jit_solution(12476536760560780529)
XLA Ops:
  0.6 11.3 copy.32
  12.0 6.4 all-to-all-start
  18.4 184.1 %all-to-all-done = bf16[2,8,256,1024]{3,1,0,2:T(8,128)(2,1)} async-done(((bf16[2,8,256,1024]{3,1,0,2:T(8,128)(2,1)}), bf16[2,8,256,1024]{3,1,0,2:T(8,128)(2,1)}, u32[]{:S(2)}, u32[]{:S(2)}) %all-to-all-start) | async-done | bytes 8388640 | tf_op jit(solution)/shard_map/all_to_all | solution.py:26
  202.5 4.2 fusion.42
  210.0 4.3 copy.49
  217.5 4.3 copy.50
  221.8 1072.9 %while.12 = (s32[]{:T(128)}, bf16[8,2,512,512]{3,2,0,1:T(8,128)(2,1)}, s32[8,512]{1,0:T(8,128)S(1)}, bf16[512,4096]{1,0:T(8,128)(2,1)}, bf16[512,4096]{1,0:T(8,128)(2,1)}, /*index=5*/s32[]{:T(128)}) while((s32[]{:T(128)}, bf16[8,2,512,512]{3,2,0,1:T(8,128)(2,1)}, s32[8,512]{1,0:T(8,128)S(1)}, bf16[512,4096]{1,0:T(8,128)(2,1)}, ...), condition=%wide.region_1.2_spmd, body=%wide.region_0.1_spmd.sunk | while | flops 8719433728 | bytes 57684108 | solution.py:43
  234.5 35.6 %fusion.62 = f32[512,512]{1,0:T(8,128)S(1)} fusion(bf16[512,4096]{1,0:T(8,128)(2,1)} %get-tuple-element.138, s32[512]{0:T(512)S(1)} %bitcast.68), kind=kOutput, calls=%fused_computation.13.clone.1 | convolution fusion | flops 2178940928 | bytes 5244928 | tf_op jit(solution)/shard_map/while/body/eval_jaxpr/tm,rt->mr/dot_general | solution.py:35
  270.1 31.8 %fusion.63 = bf16[1,1,512,512]{3,2,1,0:T(8,128)(2,1)S(1)} fusion(f32[512,512]{1,0:T(8,128)S(1)} %fusion.62, bf16[512,4096]{1,0:T(8,128)(2,1)S(1)} %copy-done.1, s32[512]{0:T(512)S(1)} %bitcast.69), kind=kOutput, calls=%fused_computation.23.clone.1 | convolution fusion | flops 2179727360 | bytes 5769216 | tf_op jit(solution)/shard_map/while/body/eval_jaxpr/tm,rt->mr/dot_general | solution.py:35
  301.9 31.1 %fusion.64 = f32[512,512]{1,0:T(8,128)S(1)} fusion(bf16[512,4096]{1,0:T(8,128)(2,1)S(1)} %copy-done.1, s32[512]{0:T(512)S(1)} %bitcast.70), kind=kOutput, calls=%fused_computation.14.clone.1 | convolution fusion | flops 2178940928 | bytes 5244928 | tf_op jit(solution)/shard_map/while/body/eval_jaxpr/tm,rt->mr/dot_general | solution.py:35
  333.0 31.5 %fusion.65 = bf16[1,1,512,512]{3,2,1,0:T(8,128)(2,1)S(1)} fusion(f32[512,512]{1,0:T(8,128)S(1)} %fusion.64, bf16[512,4096]{1,0:T(8,128)(2,1)S(1)} %copy-done.2, s32[512]{0:T(512)S(1)} %bitcast.71), kind=kOutput, calls=%fused_computation.24.clone.1 | convolution fusion | flops 2179727360 | bytes 5769216 | tf_op jit(solution)/shard_map/while/body/eval_jaxpr/tm,rt->mr/dot_general | solution.py:35
  366.0 35.6 %fusion.62 = f32[512,512]{1,0:T(8,128)S(1)} fusion(bf16[512,4096]{1,0:T(8,128)(2,1)} %get-tuple-element.138, s32[512]{0:T(512)S(1)} %bitcast.68), kind=kOutput, calls=%fused_computation.13.clone.1 | convolution fusion | flops 2178940928 | bytes 5244928 | tf_op jit(solution)/shard_map/while/body/eval_jaxpr/tm,rt->mr/dot_general | solution.py:35
  401.6 31.6 %fusion.63 = bf16[1,1,512,512]{3,2,1,0:T(8,128)(2,1)S(1)} fusion(f32[512,512]{1,0:T(8,128)S(1)} %fusion.62, bf16[512,4096]{1,0:T(8,128)(2,1)S(1)} %copy-done.1, s32[512]{0:T(512)S(1)} %bitcast.69), kind=kOutput, calls=%fused_computation.23.clone.1 | convolution fusion | flops 2179727360 | bytes 5769216 | tf_op jit(solution)/shard_map/while/body/eval_jaxpr/tm,rt->mr/dot_general | solution.py:35
  433.2 31.1 %fusion.64 = f32[512,512]{1,0:T(8,128)S(1)} fusion(bf16[512,4096]{1,0:T(8,128)(2,1)S(1)} %copy-done.1, s32[512]{0:T(512)S(1)} %bitcast.70), kind=kOutput, calls=%fused_computation.14.clone.1 | convolution fusion | flops 2178940928 | bytes 5244928 | tf_op jit(solution)/shard_map/while/body/eval_jaxpr/tm,rt->mr/dot_general | solution.py:35
  464.3 31.8 %fusion.65 = bf16[1,1,512,512]{3,2,1,0:T(8,128)(2,1)S(1)} fusion(f32[512,512]{1,0:T(8,128)S(1)} %fusion.64, bf16[512,4096]{1,0:T(8,128)(2,1)S(1)} %copy-done.2, s32[512]{0:T(512)S(1)} %bitcast.71), kind=kOutput, calls=%fused_computation.24.clone.1 | convolution fusion | flops 2179727360 | bytes 5769216 | tf_op jit(solution)/shard_map/while/body/eval_jaxpr/tm,rt->mr/dot_general | solution.py:35
  497.3 35.6 %fusion.62 = f32[512,512]{1,0:T(8,128)S(1)} fusion(bf16[512,4096]{1,0:T(8,128)(2,1)} %get-tuple-element.138, s32[512]{0:T(512)S(1)} %bitcast.68), kind=kOutput, calls=%fused_computation.13.clone.1 | convolution fusion | flops 2178940928 | bytes 5244928 | tf_op jit(solution)/shard_map/while/body/eval_jaxpr/tm,rt->mr/dot_general | solution.py:35
  532.9 31.8 %fusion.63 = bf16[1,1,512,512]{3,2,1,0:T(8,128)(2,1)S(1)} fusion(f32[512,512]{1,0:T(8,128)S(1)} %fusion.62, bf16[512,4096]{1,0:T(8,128)(2,1)S(1)} %copy-done.1, s32[512]{0:T(512)S(1)} %bitcast.69), kind=kOutput, calls=%fused_computation.23.clone.1 | convolution fusion | flops 2179727360 | bytes 5769216 | tf_op jit(solution)/shard_map/while/body/eval_jaxpr/tm,rt->mr/dot_general | solution.py:35
  564.7 31.1 %fusion.64 = f32[512,512]{1,0:T(8,128)S(1)} fusion(bf16[512,4096]{1,0:T(8,128)(2,1)S(1)} %copy-done.1, s32[512]{0:T(512)S(1)} %bitcast.70), kind=kOutput, calls=%fused_computation.14.clone.1 | convolution fusion | flops 2178940928 | bytes 5244928 | tf_op jit(solution)/shard_map/while/body/eval_jaxpr/tm,rt->mr/dot_general | solution.py:35
  595.8 31.5 %fusion.65 = bf16[1,1,512,512]{3,2,1,0:T(8,128)(2,1)S(1)} fusion(f32[512,512]{1,0:T(8,128)S(1)} %fusion.64, bf16[512,4096]{1,0:T(8,128)(2,1)S(1)} %copy-done.2, s32[512]{0:T(512)S(1)} %bitcast.71), kind=kOutput, calls=%fused_computation.24.clone.1 | convolution fusion | flops 2179727360 | bytes 5769216 | tf_op jit(solution)/shard_map/while/body/eval_jaxpr/tm,rt->mr/dot_general | solution.py:35
  628.8 35.6 %fusion.62 = f32[512,512]{1,0:T(8,128)S(1)} fusion(bf16[512,4096]{1,0:T(8,128)(2,1)} %get-tuple-element.138, s32[512]{0:T(512)S(1)} %bitcast.68), kind=kOutput, calls=%fused_computation.13.clone.1 | convolution fusion | flops 2178940928 | bytes 5244928 | tf_op jit(solution)/shard_map/while/body/eval_jaxpr/tm,rt->mr/dot_general | solution.py:35
  664.4 31.6 %fusion.63 = bf16[1,1,512,512]{3,2,1,0:T(8,128)(2,1)S(1)} fusion(f32[512,512]{1,0:T(8,128)S(1)} %fusion.62, bf16[512,4096]{1,0:T(8,128)(2,1)S(1)} %copy-done.1, s32[512]{0:T(512)S(1)} %bitcast.69), kind=kOutput, calls=%fused_computation.23.clone.1 | convolution fusion | flops 2179727360 | bytes 5769216 | tf_op jit(solution)/shard_map/while/body/eval_jaxpr/tm,rt->mr/dot_general | solution.py:35
  696.0 31.1 %fusion.64 = f32[512,512]{1,0:T(8,128)S(1)} fusion(bf16[512,4096]{1,0:T(8,128)(2,1)S(1)} %copy-done.1, s32[512]{0:T(512)S(1)} %bitcast.70), kind=kOutput, calls=%fused_computation.14.clone.1 | convolution fusion | flops 2178940928 | bytes 5244928 | tf_op jit(solution)/shard_map/while/body/eval_jaxpr/tm,rt->mr/dot_general | solution.py:35
  727.1 31.8 %fusion.65 = bf16[1,1,512,512]{3,2,1,0:T(8,128)(2,1)S(1)} fusion(f32[512,512]{1,0:T(8,128)S(1)} %fusion.64, bf16[512,4096]{1,0:T(8,128)(2,1)S(1)} %copy-done.2, s32[512]{0:T(512)S(1)} %bitcast.71), kind=kOutput, calls=%fused_computation.24.clone.1 | convolution fusion | flops 2179727360 | bytes 5769216 | tf_op jit(solution)/shard_map/while/body/eval_jaxpr/tm,rt->mr/dot_general | solution.py:35
  760.1 35.6 %fusion.62 = f32[512,512]{1,0:T(8,128)S(1)} fusion(bf16[512,4096]{1,0:T(8,128)(2,1)} %get-tuple-element.138, s32[512]{0:T(512)S(1)} %bitcast.68), kind=kOutput, calls=%fused_computation.13.clone.1 | convolution fusion | flops 2178940928 | bytes 5244928 | tf_op jit(solution)/shard_map/while/body/eval_jaxpr/tm,rt->mr/dot_general | solution.py:35
  795.7 31.8 %fusion.63 = bf16[1,1,512,512]{3,2,1,0:T(8,128)(2,1)S(1)} fusion(f32[512,512]{1,0:T(8,128)S(1)} %fusion.62, bf16[512,4096]{1,0:T(8,128)(2,1)S(1)} %copy-done.1, s32[512]{0:T(512)S(1)} %bitcast.69), kind=kOutput, calls=%fused_computation.23.clone.1 | convolution fusion | flops 2179727360 | bytes 5769216 | tf_op jit(solution)/shard_map/while/body/eval_jaxpr/tm,rt->mr/dot_general | solution.py:35
  827.5 31.1 %fusion.64 = f32[512,512]{1,0:T(8,128)S(1)} fusion(bf16[512,4096]{1,0:T(8,128)(2,1)S(1)} %copy-done.1, s32[512]{0:T(512)S(1)} %bitcast.70), kind=kOutput, calls=%fused_computation.14.clone.1 | convolution fusion | flops 2178940928 | bytes 5244928 | tf_op jit(solution)/shard_map/while/body/eval_jaxpr/tm,rt->mr/dot_general | solution.py:35
  858.6 31.5 %fusion.65 = bf16[1,1,512,512]{3,2,1,0:T(8,128)(2,1)S(1)} fusion(f32[512,512]{1,0:T(8,128)S(1)} %fusion.64, bf16[512,4096]{1,0:T(8,128)(2,1)S(1)} %copy-done.2, s32[512]{0:T(512)S(1)} %bitcast.71), kind=kOutput, calls=%fused_computation.24.clone.1 | convolution fusion | flops 2179727360 | bytes 5769216 | tf_op jit(solution)/shard_map/while/body/eval_jaxpr/tm,rt->mr/dot_general | solution.py:35
  891.6 35.6 %fusion.62 = f32[512,512]{1,0:T(8,128)S(1)} fusion(bf16[512,4096]{1,0:T(8,128)(2,1)} %get-tuple-element.138, s32[512]{0:T(512)S(1)} %bitcast.68), kind=kOutput, calls=%fused_computation.13.clone.1 | convolution fusion | flops 2178940928 | bytes 5244928 | tf_op jit(solution)/shard_map/while/body/eval_jaxpr/tm,rt->mr/dot_general | solution.py:35
  927.2 31.6 %fusion.63 = bf16[1,1,512,512]{3,2,1,0:T(8,128)(2,1)S(1)} fusion(f32[512,512]{1,0:T(8,128)S(1)} %fusion.62, bf16[512,4096]{1,0:T(8,128)(2,1)S(1)} %copy-done.1, s32[512]{0:T(512)S(1)} %bitcast.69), kind=kOutput, calls=%fused_computation.23.clone.1 | convolution fusion | flops 2179727360 | bytes 5769216 | tf_op jit(solution)/shard_map/while/body/eval_jaxpr/tm,rt->mr/dot_general | solution.py:35
  958.8 31.1 %fusion.64 = f32[512,512]{1,0:T(8,128)S(1)} fusion(bf16[512,4096]{1,0:T(8,128)(2,1)S(1)} %copy-done.1, s32[512]{0:T(512)S(1)} %bitcast.70), kind=kOutput, calls=%fused_computation.14.clone.1 | convolution fusion | flops 2178940928 | bytes 5244928 | tf_op jit(solution)/shard_map/while/body/eval_jaxpr/tm,rt->mr/dot_general | solution.py:35
  989.9 31.8 %fusion.65 = bf16[1,1,512,512]{3,2,1,0:T(8,128)(2,1)S(1)} fusion(f32[512,512]{1,0:T(8,128)S(1)} %fusion.64, bf16[512,4096]{1,0:T(8,128)(2,1)S(1)} %copy-done.2, s32[512]{0:T(512)S(1)} %bitcast.71), kind=kOutput, calls=%fused_computation.24.clone.1 | convolution fusion | flops 2179727360 | bytes 5769216 | tf_op jit(solution)/shard_map/while/body/eval_jaxpr/tm,rt->mr/dot_general | solution.py:35
  1022.9 35.6 %fusion.62 = f32[512,512]{1,0:T(8,128)S(1)} fusion(bf16[512,4096]{1,0:T(8,128)(2,1)} %get-tuple-element.138, s32[512]{0:T(512)S(1)} %bitcast.68), kind=kOutput, calls=%fused_computation.13.clone.1 | convolution fusion | flops 2178940928 | bytes 5244928 | tf_op jit(solution)/shard_map/while/body/eval_jaxpr/tm,rt->mr/dot_general | solution.py:35
  1058.5 31.8 %fusion.63 = bf16[1,1,512,512]{3,2,1,0:T(8,128)(2,1)S(1)} fusion(f32[512,512]{1,0:T(8,128)S(1)} %fusion.62, bf16[512,4096]{1,0:T(8,128)(2,1)S(1)} %copy-done.1, s32[512]{0:T(512)S(1)} %bitcast.69), kind=kOutput, calls=%fused_computation.23.clone.1 | convolution fusion | flops 2179727360 | bytes 5769216 | tf_op jit(solution)/shard_map/while/body/eval_jaxpr/tm,rt->mr/dot_general | solution.py:35
  1090.3 31.1 %fusion.64 = f32[512,512]{1,0:T(8,128)S(1)} fusion(bf16[512,4096]{1,0:T(8,128)(2,1)S(1)} %copy-done.1, s32[512]{0:T(512)S(1)} %bitcast.70), kind=kOutput, calls=%fused_computation.14.clone.1 | convolution fusion | flops 2178940928 | bytes 5244928 | tf_op jit(solution)/shard_map/while/body/eval_jaxpr/tm,rt->mr/dot_general | solution.py:35
  1121.4 31.5 %fusion.65 = bf16[1,1,512,512]{3,2,1,0:T(8,128)(2,1)S(1)} fusion(f32[512,512]{1,0:T(8,128)S(1)} %fusion.64, bf16[512,4096]{1,0:T(8,128)(2,1)S(1)} %copy-done.2, s32[512]{0:T(512)S(1)} %bitcast.71), kind=kOutput, calls=%fused_computation.24.clone.1 | convolution fusion | flops 2179727360 | bytes 5769216 | tf_op jit(solution)/shard_map/while/body/eval_jaxpr/tm,rt->mr/dot_general | solution.py:35
  1154.4 35.6 %fusion.62 = f32[512,512]{1,0:T(8,128)S(1)} fusion(bf16[512,4096]{1,0:T(8,128)(2,1)} %get-tuple-element.138, s32[512]{0:T(512)S(1)} %bitcast.68), kind=kOutput, calls=%fused_computation.13.clone.1 | convolution fusion | flops 2178940928 | bytes 5244928 | tf_op jit(solution)/shard_map/while/body/eval_jaxpr/tm,rt->mr/dot_general | solution.py:35
  1190.0 31.5 %fusion.63 = bf16[1,1,512,512]{3,2,1,0:T(8,128)(2,1)S(1)} fusion(f32[512,512]{1,0:T(8,128)S(1)} %fusion.62, bf16[512,4096]{1,0:T(8,128)(2,1)S(1)} %copy-done.1, s32[512]{0:T(512)S(1)} %bitcast.69), kind=kOutput, calls=%fused_computation.23.clone.1 | convolution fusion | flops 2179727360 | bytes 5769216 | tf_op jit(solution)/shard_map/while/body/eval_jaxpr/tm,rt->mr/dot_general | solution.py:35
  1221.6 31.1 %fusion.64 = f32[512,512]{1,0:T(8,128)S(1)} fusion(bf16[512,4096]{1,0:T(8,128)(2,1)S(1)} %copy-done.1, s32[512]{0:T(512)S(1)} %bitcast.70), kind=kOutput, calls=%fused_computation.14.clone.1 | convolution fusion | flops 2178940928 | bytes 5244928 | tf_op jit(solution)/shard_map/while/body/eval_jaxpr/tm,rt->mr/dot_general | solution.py:35
  1252.7 31.8 %fusion.65 = bf16[1,1,512,512]{3,2,1,0:T(8,128)(2,1)S(1)} fusion(f32[512,512]{1,0:T(8,128)S(1)} %fusion.64, bf16[512,4096]{1,0:T(8,128)(2,1)S(1)} %copy-done.2, s32[512]{0:T(512)S(1)} %bitcast.71), kind=kOutput, calls=%fused_computation.24.clone.1 | convolution fusion | flops 2179727360 | bytes 5769216 | tf_op jit(solution)/shard_map/while/body/eval_jaxpr/tm,rt->mr/dot_general | solution.py:35
  1294.7 16.4 %copy.36 = bf16[2,4096,512]{2,0,1:T(2,128)(2,1)} copy(bf16[2,4096,512]{2,1,0:T(8,128)(2,1)} %bitcast.65) | data formatting | bytes 16777216 | tf_op jit(solution)/shard_map/reshape | solution.py:44
  1318.5 182.6 %all-to-all-done.1 = bf16[2,4096,512]{2,0,1:T(2,128)(2,1)} async-done(((bf16[2,4096,512]{2,0,1:T(2,128)(2,1)}), bf16[2,4096,512]{2,0,1:T(2,128)(2,1)}, u32[]{:S(2)}, u32[]{:S(2)}) %all-to-all-start.1) | async-done | bytes 8388640 | tf_op jit(solution)/shard_map/all_to_all | solution.py:48
  1501.1 8.0 copy.37
  1509.0 12.0 copy.38
  1521.0 9.6 copy.39
  1530.6 8.5 bitcast_select_fusion
  1539.2 12.5 copy.40
  1551.7 15.8 fusion.43
  1570.4 37.0 %psum.7 = f32[8,1024]{1,0:T(8,128)S(1)} all-reduce(f32[8,1024]{1,0:T(8,128)S(1)} %fusion.39), channel_id=1, replica_groups=mesh['grp'=4,'wide'=8] {'grp','wide'}, use_global_device_ids=true, to_apply=%region_3.4 | all-reduce | flops 8192 | bytes 65536 | tf_op jit(solution)/shard_map/psum | solution.py:66
  (72 shorter events, 25.9 us)
Async XLA Ops:
  0.6 1315.8 %copy-start = (s32[4096]{0:T(1024)S(1)}, s32[4096]{0:T(1024)}, u32[]{:S(2)}) copy-start(s32[4096]{0:T(1024)} %param.9) | copy-start | bytes 49156
  12.0 6.5 copy-start.4
  12.0 190.5 %all-to-all-start = ((bf16[2,8,256,1024]{3,1,0,2:T(8,128)(2,1)}), bf16[2,8,256,1024]{3,1,0,2:T(8,128)(2,1)}, u32[]{:S(2)}, u32[]{:S(2)}) async-start(bf16[2,8,256,1024]{3,1,0,2:T(8,128)(2,1)} %copy.32), calls=%async_computation | async-start | bytes 16777216 | tf_op jit(solution)/shard_map/all_to_all | solution.py:26
  234.5 35.6 %copy-start.1 = (bf16[512,4096]{1,0:T(8,128)(2,1)S(1)}, bf16[512,4096]{1,0:T(8,128)(2,1)}, u32[]{:S(2)}) copy-start(bf16[512,4096]{1,0:T(8,128)(2,1)} %get-tuple-element.137) | copy-start | bytes 12582916 | tf_op jit(solution)/shard_map/while
  301.9 31.1 %copy-start.2 = (bf16[512,4096]{1,0:T(8,128)(2,1)S(1)}, bf16[512,4096]{1,0:T(8,128)(2,1)}, u32[]{:S(2)}) copy-start(bf16[512,4096]{1,0:T(8,128)(2,1)} %get-tuple-element.138) | copy-start | bytes 12582916 | tf_op jit(solution)/shard_map/while
  366.0 35.6 %copy-start.1 = (bf16[512,4096]{1,0:T(8,128)(2,1)S(1)}, bf16[512,4096]{1,0:T(8,128)(2,1)}, u32[]{:S(2)}) copy-start(bf16[512,4096]{1,0:T(8,128)(2,1)} %get-tuple-element.137) | copy-start | bytes 12582916 | tf_op jit(solution)/shard_map/while
  433.2 31.1 %copy-start.2 = (bf16[512,4096]{1,0:T(8,128)(2,1)S(1)}, bf16[512,4096]{1,0:T(8,128)(2,1)}, u32[]{:S(2)}) copy-start(bf16[512,4096]{1,0:T(8,128)(2,1)} %get-tuple-element.138) | copy-start | bytes 12582916 | tf_op jit(solution)/shard_map/while
  497.3 35.6 %copy-start.1 = (bf16[512,4096]{1,0:T(8,128)(2,1)S(1)}, bf16[512,4096]{1,0:T(8,128)(2,1)}, u32[]{:S(2)}) copy-start(bf16[512,4096]{1,0:T(8,128)(2,1)} %get-tuple-element.137) | copy-start | bytes 12582916 | tf_op jit(solution)/shard_map/while
  564.7 31.1 %copy-start.2 = (bf16[512,4096]{1,0:T(8,128)(2,1)S(1)}, bf16[512,4096]{1,0:T(8,128)(2,1)}, u32[]{:S(2)}) copy-start(bf16[512,4096]{1,0:T(8,128)(2,1)} %get-tuple-element.138) | copy-start | bytes 12582916 | tf_op jit(solution)/shard_map/while
  628.8 35.6 %copy-start.1 = (bf16[512,4096]{1,0:T(8,128)(2,1)S(1)}, bf16[512,4096]{1,0:T(8,128)(2,1)}, u32[]{:S(2)}) copy-start(bf16[512,4096]{1,0:T(8,128)(2,1)} %get-tuple-element.137) | copy-start | bytes 12582916 | tf_op jit(solution)/shard_map/while
  696.0 31.1 %copy-start.2 = (bf16[512,4096]{1,0:T(8,128)(2,1)S(1)}, bf16[512,4096]{1,0:T(8,128)(2,1)}, u32[]{:S(2)}) copy-start(bf16[512,4096]{1,0:T(8,128)(2,1)} %get-tuple-element.138) | copy-start | bytes 12582916 | tf_op jit(solution)/shard_map/while
  760.1 35.6 %copy-start.1 = (bf16[512,4096]{1,0:T(8,128)(2,1)S(1)}, bf16[512,4096]{1,0:T(8,128)(2,1)}, u32[]{:S(2)}) copy-start(bf16[512,4096]{1,0:T(8,128)(2,1)} %get-tuple-element.137) | copy-start | bytes 12582916 | tf_op jit(solution)/shard_map/while
  827.5 31.1 %copy-start.2 = (bf16[512,4096]{1,0:T(8,128)(2,1)S(1)}, bf16[512,4096]{1,0:T(8,128)(2,1)}, u32[]{:S(2)}) copy-start(bf16[512,4096]{1,0:T(8,128)(2,1)} %get-tuple-element.138) | copy-start | bytes 12582916 | tf_op jit(solution)/shard_map/while
  891.6 35.6 %copy-start.1 = (bf16[512,4096]{1,0:T(8,128)(2,1)S(1)}, bf16[512,4096]{1,0:T(8,128)(2,1)}, u32[]{:S(2)}) copy-start(bf16[512,4096]{1,0:T(8,128)(2,1)} %get-tuple-element.137) | copy-start | bytes 12582916 | tf_op jit(solution)/shard_map/while
  958.8 31.1 %copy-start.2 = (bf16[512,4096]{1,0:T(8,128)(2,1)S(1)}, bf16[512,4096]{1,0:T(8,128)(2,1)}, u32[]{:S(2)}) copy-start(bf16[512,4096]{1,0:T(8,128)(2,1)} %get-tuple-element.138) | copy-start | bytes 12582916 | tf_op jit(solution)/shard_map/while
  1022.9 35.6 %copy-start.1 = (bf16[512,4096]{1,0:T(8,128)(2,1)S(1)}, bf16[512,4096]{1,0:T(8,128)(2,1)}, u32[]{:S(2)}) copy-start(bf16[512,4096]{1,0:T(8,128)(2,1)} %get-tuple-element.137) | copy-start | bytes 12582916 | tf_op jit(solution)/shard_map/while
  1090.3 31.1 %copy-start.2 = (bf16[512,4096]{1,0:T(8,128)(2,1)S(1)}, bf16[512,4096]{1,0:T(8,128)(2,1)}, u32[]{:S(2)}) copy-start(bf16[512,4096]{1,0:T(8,128)(2,1)} %get-tuple-element.138) | copy-start | bytes 12582916 | tf_op jit(solution)/shard_map/while
  1154.4 35.6 %copy-start.1 = (bf16[512,4096]{1,0:T(8,128)(2,1)S(1)}, bf16[512,4096]{1,0:T(8,128)(2,1)}, u32[]{:S(2)}) copy-start(bf16[512,4096]{1,0:T(8,128)(2,1)} %get-tuple-element.137) | copy-start | bytes 12582916 | tf_op jit(solution)/shard_map/while
  1221.6 31.1 %copy-start.2 = (bf16[512,4096]{1,0:T(8,128)(2,1)S(1)}, bf16[512,4096]{1,0:T(8,128)(2,1)}, u32[]{:S(2)}) copy-start(bf16[512,4096]{1,0:T(8,128)(2,1)} %get-tuple-element.138) | copy-start | bytes 12582916 | tf_op jit(solution)/shard_map/while
  1311.1 3.9 copy-start.3
  1311.1 190.0 %all-to-all-start.1 = ((bf16[2,4096,512]{2,0,1:T(2,128)(2,1)}), bf16[2,4096,512]{2,0,1:T(2,128)(2,1)}, u32[]{:S(2)}, u32[]{:S(2)}) async-start(bf16[2,4096,512]{2,0,1:T(2,128)(2,1)} %copy.36), calls=%async_computation.1 | async-start | bytes 16777216 | tf_op jit(solution)/shard_map/all_to_all | solution.py:48
where the time goes:
time: 1610 us
  matrix products  1060 us (66%)
  waiting for transfers between devices  367 us (23%)
  local copies, waits for them, and re-layouts  93.1 us (6%)
  blocking collectives  37 us (2%)
  loops' own time  24.5 us (2%)
  other arithmetic  18.6 us (1%)
    dot_general x32, matrix products, product(): jnp.einsum('tm,rt->mr', table, values, preferred_element_type=jnp.float32)  1040 us
    all_to_all x1, waiting for transfers between devices, body(): lax.all_to_all(visibilities, 'grp', split_axis=2, concat_axis=3, tiled=True)  184 us
    all_to_all x1, waiting for transfers between devices, body(): lax.all_to_all(spectrum, ('grp', 'wide'), split_axis=1, concat_axis=2, ti...  183 us
    psum x1, blocking collectives, body(): totals = lax.psum(partial_sums, ('grp', 'wide'))  37 us
  transfers between devices with their start and end apart: 2, of which 2 were waited for; matrix products, arithmetic and copies ran while one was open for 0% of the time, Pallas kernels for 0%

commit v1 on v0

v1 whole, which is shorter than its diff:
```python
import math

import jax
import jax.numpy as jnp
import ml_dtypes
import numpy as np
from jax import lax
from jax.sharding import PartitionSpec as P


def factors(times):
    first = 1
    while first * first < times:
        first *= 2
    return first, times // first


def rotation(angles):
    cos, sin = np.cos(angles), np.sin(angles)
    return np.stack([np.stack([cos, sin]), np.stack([-sin, cos])]).astype(ml_dtypes.bfloat16)


def tables(times):
    n1, n2 = factors(times)
    one, two = np.arange(n1), np.arange(n2)
    first = rotation(2.0 * np.pi * (one[:, None] * one[None, :] % n1) / n1)
    modes = one[:, None, None] + n1 * two[None, :, None]
    second = rotation(2.0 * np.pi * (two[None, None, :] * modes % times) / times)
    return first, second


def body(visibilities, filters, counts, m_of_slot, band_of_block):
    highest = lax.Precision.HIGHEST
    channels = visibilities.shape[1]
    groups = lax.axis_size("grp")
    wides = lax.axis_size("wide")
    times = visibilities.shape[3] * groups
    slots, modes_kept, baselines = filters.shape
    blocks = band_of_block.shape[1]
    n1, n2 = factors(times)
    first, second = tables(times)
    local = lax.all_to_all(visibilities, "grp", split_axis=2, concat_axis=3, tiled=True)
    base_dev = local.shape[2]
    rows = channels * base_dev
    samples = local.reshape(2, rows, n1, n2)
    half = jnp.einsum("yxma,xrab->mbyr", first, samples, preferred_element_type=jnp.float32)
    half = (half * (1.0 / math.sqrt(times))).astype(jnp.bfloat16)
    spectrum = jnp.einsum("zymnb,mbyr->mnzr", second, half, preferred_element_type=jnp.float32)
    spectrum = spectrum.astype(jnp.bfloat16).reshape(times, 2 * rows)
    place_of_slot = (m_of_slot % n1) * n2 + m_of_slot // n1
    ordered = jnp.take(spectrum, place_of_slot, axis=0, mode="clip")
    ordered = ordered.reshape(groups * wides, slots, 2 * rows)
    moved = lax.all_to_all(ordered, ("grp", "wide"), split_axis=0, concat_axis=0, tiled=True)
    owned = moved.reshape(groups, wides, slots, 2, channels, base_dev).transpose(2, 3, 4, 1, 0, 5)
    owned = owned.reshape(slots, 2, channels, baselines)
    place = lax.axis_index(("grp", "wide"))
    mine = lax.dynamic_slice_in_dim(m_of_slot, place * slots, slots)
    active_counts = counts[mine]
    band_rows = band_of_block[mine]
    active = jnp.arange(baselines, dtype=jnp.int32)[None, :] < active_counts[:, None]
    masked = jnp.where(active[:, None, None, :], owned, jnp.zeros_like(owned))
    coeffs = jnp.einsum("sxcb,skb->sxck", masked, filters, preferred_element_type=jnp.float32)
    kl_coeffs = coeffs.astype(jnp.bfloat16)
    power = coeffs[:, 0] * coeffs[:, 0] + coeffs[:, 1] * coeffs[:, 1]
    block_power = power.reshape(slots, channels, blocks, modes_kept // blocks).sum(axis=-1)
    bands = BANDS
    one_hot = (band_rows[:, :, None] == jnp.arange(bands, dtype=jnp.int32)[None, None, :]).astype(
        jnp.float32
    )
    partial_sums = jnp.einsum("scj,sjn->cn", block_power, one_hot, precision=highest)
    band_scale = bands / (times * modes_kept)
    totals = lax.psum(partial_sums, ("grp", "wide"))
    band_dev = bands // (groups * wides)
    band_power = lax.dynamic_slice_in_dim(totals, place * band_dev, band_dev, 1) * band_scale
    return (kl_coeffs, band_power)


BANDS = 1024


def solution(mesh):
    placed = (P(None, None, "wide", "grp"), P(("grp", "wide"), None, None), P(), P(), P())
    return jax.shard_map(
        body,
        mesh=mesh,
        in_specs=placed,
        out_specs=(P(("grp", "wide"), None, None, None), P(None, ("grp", "wide"))),
        check_vma=False,
    )
```

time: 1610 us -> 619 us (0.38)
  matrix products: 1060 us -> 41.9 us
  local copies, waits for them, and re-layouts: 93.1 us -> 144 us
  loops' own time: 24.5 us -> 0 us
    dot_general x32 -> x2, matrix products: 1040 us -> 24.7 us  [the longest x1 14.1 us: body(): jnp.einsum('yxma,xrab->mbyr', first, samples, preferred_element_type=jnp....]
    gather x0 -> x1, local copies, waits for them, and re-layouts: none -> 25.4 us  [body(): ordered = jnp.take(spectrum, place_of_slot, axis=0, mode='clip')]
    another operation x1 -> x0, loops' own time: 24.5 us -> none  [body(): blocks = lax.map(transform, m_of_slot.reshape(NT // mode_block, mode_block))]
    reshape x2, local copies, waits for them, and re-layouts: 16.4 us -> 34.4 us  [the longest x1 22.5 us: body(): samples = local.reshape(2, rows, n1, n2)]
    convert_element_type x0 -> x1, local copies, waits for them, and re-layouts: none -> 16.3 us  [body(): spectrum = spectrum.astype(jnp.bfloat16).reshape(times, 2 * rows)]
where the time goes in v1:
time: 619 us; the launch traced here: 612 us
  waiting for transfers between devices  367 us (59%)
  local copies, waits for them, and re-layouts  144 us (23%)
  matrix products  41.9 us (7%)
  blocking collectives  37 us (6%)
  starting transfers between devices  10.8 us (2%)
  other arithmetic  9.61 us (2%)
    all_to_all x1, waiting for transfers between devices, body(): lax.all_to_all(visibilities, 'grp', split_axis=2, concat_axis=3, tiled=True)  184 us
    all_to_all x1, waiting for transfers between devices, body(): lax.all_to_all(ordered, ('grp', 'wide'), split_axis=0, concat_axis=0, til...  183 us
    psum x1, blocking collectives, body(): totals = lax.psum(partial_sums, ('grp', 'wide'))  37 us
    gather x1, local copies, waits for them, and re-layouts, body(): ordered = jnp.take(spectrum, place_of_slot, axis=0, mode='clip')  25.4 us
    reshape x1, local copies, waits for them, and re-layouts, body(): samples = local.reshape(2, rows, n1, n2)  22.5 us
    unnamed x12, local copies, waits for them, and re-layouts  22.4 us
    all_to_all x1, local copies, waits for them, and re-layouts, body(): lax.all_to_all(visibilities, 'grp', split_axis=2, concat_axis=3, tiled=True)  21.9 us
    convert_element_type x1, local copies, waits for them, and re-layouts, body(): spectrum = spectrum.astype(jnp.bfloat16).reshape(times, 2 * rows)  16.3 us
  transfers between devices with their start and end apart: 2, of which 2 were waited for; matrix products, arithmetic and copies ran while one was open for 0% of the time, Pallas kernels for 0%

profile of v1, /device:TPU:0, one launch (start us, length us, event | category | flops | bytes accessed | tf_op | source)
XLA Modules:
  0.0 612.2 jit_solution(3224905570573762170)
XLA Ops:
  0.6 0.0 copy-start
  0.6 11.3 %copy.22 = bf16[2,8,256,1024]{3,1,0,2:T(8,128)(2,1)} copy(bf16[2,8,256,1024]{3,2,1,0:T(8,128)(2,1)} %param.7) | data formatting | bytes 16777216 | tf_op args[0]
  12.0 0.0 copy-start.3
  12.0 6.6 %all-to-all-start = ((bf16[2,8,256,1024]{3,1,0,2:T(8,128)(2,1)}), bf16[2,8,256,1024]{3,1,0,2:T(8,128)(2,1)}, u32[]{:S(2)}, u32[]{:S(2)}) async-start(bf16[2,8,256,1024]{3,1,0,2:T(8,128)(2,1)} %copy.22), calls=%async_computation | async-start | bytes 16777216 | tf_op jit(solution)/shard_map/all_to_all | solution.py:42
  18.6 0.0 copy-done.3
  18.6 184.0 %all-to-all-done = bf16[2,8,256,1024]{3,1,0,2:T(8,128)(2,1)} async-done(((bf16[2,8,256,1024]{3,1,0,2:T(8,128)(2,1)}), bf16[2,8,256,1024]{3,1,0,2:T(8,128)(2,1)}, u32[]{:S(2)}, u32[]{:S(2)}) %all-to-all-start) | async-done | bytes 8388640 | tf_op jit(solution)/shard_map/all_to_all | solution.py:42
  202.7 21.9 %copy.23 = bf16[2,8,4,64,1024]{3,1,4,2,0:T(8,128)(2,1)} copy(bf16[2,8,4,64,1024]{4,1,0,3,2:T(8,128)(2,1)} %bitcast.2) | data formatting | bytes 16777216 | tf_op jit(solution)/shard_map/all_to_all | solution.py:42
  224.5 0.0 copy-start.2
  224.5 22.5 %reshape.44 = bf16[2,512,64,64]{1,3,2,0:T(8,128)(2,1)} reshape(bf16[2,8,64,4,1024]{2,1,4,3,0:T(8,128)(2,1)} %bitcast.56) | data formatting | bytes 16777216 | tf_op jit(solution)/shard_map/reshape | solution.py:45
  247.1 0.0 copy-done.2
  247.1 14.1 %fusion.3 = bf16[64,64,2,512,1]{3,0,1,2,4:T(8,128)(2,1)S(1)} fusion(bf16[2,2,64,64,1]{3,2,1,4,0:T(8,128)(2,1)S(1)} %copy-done.2, bf16[2,512,64,64]{1,3,2,0:T(8,128)(2,1)} %reshape.44), kind=kOutput, calls=%fused_computation.8 | convolution fusion | flops 1082130432 | bytes 16809984 | tf_op jit(solution)/shard_map/yxma,xrab->mbyr/dot_general | solution.py:46
  261.2 10.6 %fusion.10 = bf16[64,64,2,512]{3,1,2,0:T(8,128)(2,1)} fusion(bf16[2,2,64,64,64]{4,3,1,0,2:T(8,128)(2,1)} %constant.63.clone, bf16[64,64,2,512,1]{3,0,1,2,4:T(8,128)(2,1)S(1)} %fusion.3), kind=kOutput, calls=%fused_computation.14 | convolution fusion | flops 1077936128 | bytes 18874368 | tf_op jit(solution)/shard_map/zymnb,mbyr->mnzr/dot_general | solution.py:48
  271.8 16.3 %copy.26 = bf16[64,64,2,512]{3,2,1,0:T(2,128)(2,1)} copy(bf16[64,64,2,512]{3,1,2,0:T(8,128)(2,1)} %fusion.10) | data formatting | bytes 16777216 | tf_op jit(solution)/shard_map/convert_element_type | solution.py:49
  288.1 9.3 %copy.42 = bf16[512,8,2,512]{3,1,2,0:T(8,128)(2,1)} copy(bf16[512,8,2,512]{3,2,1,0:T(2,128)(2,1)} %bitcast.58) | data formatting | bytes 16777216
  297.4 25.4 %gather_fusion.1 = bf16[4096,1024]{1,0:T(8,128)(2,1)} fusion(bf16[4096,1024]{1,0:T(8,128)(2,1)} %bitcast.55, s32[4096]{0:T(1024)S(1)} %fusion.20), kind=kCustom, calls=%fused_computation.1 | custom fusion | bytes 16793600 | tf_op jit(solution)/shard_map/jit(_take)/gather | solution.py:51
  322.7 11.9 %copy.27 = bf16[32,128,1024]{1,2,0:T(8,128)(2,1)} copy(bf16[32,128,1024]{2,1,0:T(8,128)(2,1)} %bitcast.57) | data formatting | bytes 16777216 | tf_op jit(solution)/shard_map/reshape | solution.py:52
  334.7 0.0 copy-start.1
  334.7 4.1 all-to-all-start.1
  338.8 0.0 copy-done.1
  338.8 0.6 copy.31
  339.4 0.1 compare_select_fusion
  339.5 0.0 copy-done
  339.5 1.1 gather_fusion
  340.7 0.6 gather_fusion.2
  341.4 0.2 iota_compare_fusion.4
  341.6 183.3 %all-to-all-done.1 = bf16[32,128,1024]{1,2,0:T(8,128)(2,1)} async-done(((bf16[32,128,1024]{1,2,0:T(8,128)(2,1)}), bf16[32,128,1024]{1,2,0:T(8,128)(2,1)}, u32[]{:S(2)}, u32[]{:S(2)}) %all-to-all-start.1) | async-done | bytes 8388640 | tf_op jit(solution)/shard_map/all_to_all | solution.py:53
  524.8 9.6 %copy.28 = bf16[128,2,8,8,4,64]{0,5,4,3,2,1:T(8,128)(2,1)} copy(bf16[128,2,8,8,4,64]{0,5,2,1,3,4:T(8,128)(2,1)} %bitcast.14) | data formatting | bytes 16777216 | tf_op jit(solution)/shard_map/transpose | solution.py:54
  534.5 8.5 %bitcast_select_fusion = bf16[128,2,8,2048]{0,3,2,1:T(8,128)(2,1)} fusion(bf16[128,2,8,8,4,64]{0,5,4,3,2,1:T(8,128)(2,1)} %copy.28, pred[128,2048]{0,1:T(8,128)(4,1)S(1)} %iota_compare_fusion.4), kind=kLoop, calls=%fused_computation.9 | loop fusion | flops 4194304 | bytes 17039360 | tf_op jit(solution)/shard_map/jit(_where)/select_n | solution.py:61
  543.0 12.4 %copy.29 = bf16[128,2,8,2048]{3,2,1,0:T(8,128)(2,1)} copy(bf16[128,2,8,2048]{0,3,2,1:T(8,128)(2,1)} %bitcast_select_fusion) | data formatting | bytes 16777216 | tf_op jit(solution)/shard_map/jit(_where)/select_n | solution.py:61
  555.4 15.8 %fusion.25 = (bf16[128,2,8,64]{3,2,1,0:T(8,128)(2,1)S(1)}, f32[128,2,8,64]{3,2,1,0:T(8,128)S(1)}) fusion(bf16[128,2,8,2048]{3,2,1,0:T(8,128)(2,1)} %copy.29, bf16[128,64,2048]{2,1,0:T(8,128)(2,1)} %param.8), kind=kOutput, calls=%fused_computation.41 | convolution fusion | flops 537001984 | bytes 42729472 | tf_op jit(solution)/shard_map/sxcb,skb->sxck/dot_general | solution.py:62
  571.2 1.2 copy.34
  572.3 0.1 fusion.16
  572.4 0.2 copy.30
  572.6 0.1 bitcast_reduce_fusion
  572.7 1.5 fusion.15
  574.1 37.0 %psum.7 = f32[8,1024]{1,0:T(8,128)S(1)} all-reduce(f32[8,1024]{1,0:T(8,128)S(1)} %fusion.15), channel_id=1, replica_groups=mesh['grp'=4,'wide'=8] {'grp','wide'}, use_global_device_ids=true, to_apply=%region_1.2 | all-reduce | flops 8192 | bytes 65536 | tf_op jit(solution)/shard_map/psum | solution.py:72
  611.1 0.7 dynamic-slice_multiply_fusion
  (3 shorter events, 0.1 us)
Async XLA Ops:
  0.6 338.9 %copy-start = (s32[4096]{0:T(1024)S(1)}, s32[4096]{0:T(1024)}, u32[]{:S(2)}) copy-start(s32[4096]{0:T(1024)} %param.9) | copy-start | bytes 49156
  12.0 6.6 %copy-start.3 = (s32[4096]{0:T(1024)S(1)}, s32[4096]{0:T(1024)}, u32[]{:S(2)}) copy-start(s32[4096]{0:T(1024)} %param.10) | copy-start | bytes 49156
  12.0 190.7 %all-to-all-start = ((bf16[2,8,256,1024]{3,1,0,2:T(8,128)(2,1)}), bf16[2,8,256,1024]{3,1,0,2:T(8,128)(2,1)}, u32[]{:S(2)}, u32[]{:S(2)}) async-start(bf16[2,8,256,1024]{3,1,0,2:T(8,128)(2,1)} %copy.22), calls=%async_computation | async-start | bytes 16777216 | tf_op jit(solution)/shard_map/all_to_all | solution.py:42
  224.5 22.5 %copy-start.2 = (bf16[2,2,64,64,1]{3,2,1,4,0:T(8,128)(2,1)S(1)}, bf16[2,2,64,64,1]{3,2,1,4,0:T(8,128)(2,1)}, u32[]{:S(2)}) copy-start(bf16[2,2,64,64,1]{3,2,1,4,0:T(8,128)(2,1)} %constant.64) | copy-start | bytes 98308
  334.7 4.1 copy-start.1
  334.7 190.2 %all-to-all-start.1 = ((bf16[32,128,1024]{1,2,0:T(8,128)(2,1)}), bf16[32,128,1024]{1,2,0:T(8,128)(2,1)}, u32[]{:S(2)}, u32[]{:S(2)}) async-start(bf16[32,128,1024]{1,2,0:T(8,128)(2,1)} %copy.27), calls=%async_computation.1 | async-start | bytes 16777216 | tf_op jit(solution)/shard_map/all_to_all | solution.py:53

commit v2 on v1

--- a/solution.py
+++ b/solution.py
@@ -39,27 +39,47 @@
     blocks = band_of_block.shape[1]
     n1, n2 = factors(times)
     first, second = tables(times)
-    local = lax.all_to_all(visibilities, "grp", split_axis=2, concat_axis=3, tiled=True)
-    base_dev = local.shape[2]
-    rows = channels * base_dev
-    samples = local.reshape(2, rows, n1, n2)
-    half = jnp.einsum("yxma,xrab->mbyr", first, samples, preferred_element_type=jnp.float32)
-    half = (half * (1.0 / math.sqrt(times))).astype(jnp.bfloat16)
-    spectrum = jnp.einsum("zymnb,mbyr->mnzr", second, half, preferred_element_type=jnp.float32)
-    spectrum = spectrum.astype(jnp.bfloat16).reshape(times, 2 * rows)
+    ranks = groups * wides
     place_of_slot = (m_of_slot % n1) * n2 + m_of_slot // n1
-    ordered = jnp.take(spectrum, place_of_slot, axis=0, mode="clip")
-    ordered = ordered.reshape(groups * wides, slots, 2 * rows)
-    moved = lax.all_to_all(ordered, ("grp", "wide"), split_axis=0, concat_axis=0, tiled=True)
-    owned = moved.reshape(groups, wides, slots, 2, channels, base_dev).transpose(2, 3, 4, 1, 0, 5)
-    owned = owned.reshape(slots, 2, channels, baselines)
     place = lax.axis_index(("grp", "wide"))
     mine = lax.dynamic_slice_in_dim(m_of_slot, place * slots, slots)
     active_counts = counts[mine]
     band_rows = band_of_block[mine]
     active = jnp.arange(baselines, dtype=jnp.int32)[None, :] < active_counts[:, None]
-    masked = jnp.where(active[:, None, None, :], owned, jnp.zeros_like(owned))
-    coeffs = jnp.einsum("sxcb,skb->sxck", masked, filters, preferred_element_type=jnp.float32)
+    masked = jnp.where(active[:, None, :], filters, jnp.zeros_like(filters))
+    parts = 2 if channels % 2 == 0 else 1
+    part = channels // parts
+    regrouped = [
+        lax.all_to_all(
+            lax.slice_in_dim(visibilities, i * part, (i + 1) * part, axis=1),
+            "grp", split_axis=2, concat_axis=3, tiled=True,
+        )
+        for i in range(parts)
+    ]
+    base_dev = regrouped[0].shape[2]
+    rows = part * base_dev
+
+    def transform(local):
+        samples = local.reshape(2, rows, n1, n2)
+        half = jnp.einsum("yxma,xrab->mbyr", first, samples, preferred_element_type=jnp.float32)
+        half = (half * (1.0 / math.sqrt(times))).astype(jnp.bfloat16)
+        spectrum = jnp.einsum("zymnb,mbyr->mnzr", second, half, preferred_element_type=jnp.float32)
+        spectrum = spectrum.astype(jnp.bfloat16).reshape(times, 2 * rows)
+        ordered = jnp.take(spectrum, place_of_slot, axis=0, mode="clip")
+        return ordered.reshape(ranks, slots, 2 * rows)
+
+    ordered = [transform(local) for local in regrouped]
+    moved = [
+        lax.all_to_all(one, ("grp", "wide"), split_axis=0, concat_axis=0, tiled=True)
+        for one in ordered
+    ]
+
+    def filtered(one):
+        owned = one.reshape(groups, wides, slots, 2, part, base_dev).transpose(2, 3, 4, 1, 0, 5)
+        owned = owned.reshape(slots, 2, part, baselines)
+        return jnp.einsum("sxcb,skb->sxck", owned, masked, preferred_element_type=jnp.float32)
+
+    coeffs = jnp.concatenate([filtered(one) for one in moved], axis=2)
     kl_coeffs = coeffs.astype(jnp.bfloat16)
     power = coeffs[:, 0] * coeffs[:, 0] + coeffs[:, 1] * coeffs[:, 1]
     block_power = power.reshape(slots, channels, blocks, modes_kept // blocks).sum(axis=-1)
@@ -68,10 +88,10 @@
         jnp.float32
     )
     partial_sums = jnp.einsum("scj,sjn->cn", block_power, one_hot, precision=highest)
-    band_scale = bands / (times * modes_kept)
-    totals = lax.psum(partial_sums, ("grp", "wide"))
-    band_dev = bands // (groups * wides)
-    band_power = lax.dynamic_slice_in_dim(totals, place * band_dev, band_dev, 1) * band_scale
+    band_dev = bands // ranks
+    slices = partial_sums.reshape(channels, ranks, band_dev).transpose(1, 0, 2)
+    slices = lax.all_to_all(slices, ("grp", "wide"), split_axis=0, concat_axis=0, tiled=True)
+    band_power = slices.sum(axis=0) * (bands / (times * modes_kept))
     return (kl_coeffs, band_power)
 
 

time: 619 us -> 490 us (0.79)
  waiting for transfers between devices: 367 us -> 201 us
  local copies, waits for them, and re-layouts: 144 us -> 192 us
  blocking collectives: 37 us -> 0 us
  starting transfers between devices: 10.8 us -> 35.1 us
  matrix products: 41.9 us -> 50.8 us
  other arithmetic: 9.61 us -> 2.39 us
    all_to_all x2 -> x5, waiting for transfers between devices: 367 us -> 201 us  [the longest x2 101 us: body(): lax.all_to_all(lax.slice_in_dim(visibilities, i * part, (i + 1) * part, a...]
    reshape x2 -> x8, local copies, waits for them, and re-layouts: 34.4 us -> 80.2 us  [the longest x4 51.5 us: transform(): samples = local.reshape(2, rows, n1, n2)]
    psum x1 -> x0, blocking collectives: 37 us -> none  [body(): totals = lax.psum(partial_sums, ('grp', 'wide'))]
    all_to_all x2 -> x5, starting transfers between devices: 10.8 us -> 35.1 us  [the longest x2 19.7 us: body(): lax.all_to_all(one, ('grp', 'wide'), split_axis=0, concat_axis=0, tiled=T...]
    gather x1 -> x2, local copies, waits for them, and re-layouts: 25.4 us -> 40.5 us  [transform(): ordered = jnp.take(spectrum, place_of_slot, axis=0, mode='clip')]
    select_n x1 -> x0, local copies, waits for them, and re-layouts: 12.4 us -> none  [body(): masked = jnp.where(active[:, None, None, :], owned, jnp.zeros_like(owned))]
    select_n x1 -> x0, other arithmetic: 8.5 us -> none  [body(): masked = jnp.where(active[:, None, None, :], owned, jnp.zeros_like(owned))]
    all_to_all x1 -> x3, local copies, waits for them, and re-layouts: 21.9 us -> 15.3 us  [the longest x2 14.8 us: body(): lax.all_to_all(lax.slice_in_dim(visibilities, i * part, (i + 1) * part, a...]
  transfers between devices with their start and end apart: 2 -> 5, of which waited for: 2 -> 5; matrix products, arithmetic and copies ran while one was open for 0% -> 37% of each run, Pallas kernels for 0% -> 0%
where the time goes in v2:
time: 490 us; the launch traced here: 482 us
  waiting for transfers between devices  201 us (41%)
  local copies, waits for them, and re-layouts  192 us (39%)
  matrix products  50.8 us (10%)
  starting transfers between devices  35.1 us (7%)
    all_to_all x2, waiting for transfers between devices, body(): lax.all_to_all(lax.slice_in_dim(visibilities, i * part, (i + 1) * part, a...  101 us
    all_to_all x2, waiting for transfers between devices, body(): lax.all_to_all(one, ('grp', 'wide'), split_axis=0, concat_axis=0, tiled=T...  94.1 us
    reshape x4, local copies, waits for them, and re-layouts, transform(): samples = local.reshape(2, rows, n1, n2)  51.5 us
    gather x2, local copies, waits for them, and re-layouts, transform(): ordered = jnp.take(spectrum, place_of_slot, axis=0, mode='clip')  40.5 us
    dot_general x2, matrix products, filtered(): jnp.einsum('sxcb,skb->sxck', owned, masked, preferred_element_type=jnp.fl...  33.6 us
    unnamed x20, local copies, waits for them, and re-layouts  24.9 us
    all_to_all x2, starting transfers between devices, body(): lax.all_to_all(one, ('grp', 'wide'), split_axis=0, concat_axis=0, tiled=T...  19.7 us
    reshape x2, local copies, waits for them, and re-layouts, filtered(): owned = owned.reshape(slots, 2, part, baselines)  15.9 us
  transfers between devices with their start and end apart: 5, of which 5 were waited for; matrix products, arithmetic and copies ran while one was open for 37% of the time, Pallas kernels for 0%

profile of v2, /device:TPU:0, one launch (start us, length us, event | category | flops | bytes accessed | tf_op | source)
XLA Modules:
  0.0 482.4 jit_solution(8873988846153163867)
XLA Ops:
  0.6 5.3 %fusion.52 = (bf16[2,4,256,1024]{3,2,1,0:T(8,128)(2,1)}, bf16[2,4,256,1024]{3,2,1,0:T(8,128)(2,1)S(1)}) fusion(bf16[2,8,256,1024]{3,2,1,0:T(8,128)(2,1)} %param.9), kind=kLoop, calls=%fused_computation.70 | loop fusion | bytes 16777216 | tf_op jit(solution)/shard_map/slice | solution.py:54
  5.9 5.2 %copy.63 = bf16[2,4,256,1024]{3,1,0,2:T(4,128)(2,1)} copy(bf16[2,4,256,1024]{3,2,1,0:T(8,128)(2,1)S(1)} %get-tuple-element.9) | data formatting | bytes 8388608
  11.1 6.3 %all-to-all-start.2 = ((bf16[2,4,256,1024]{3,1,0,2:T(4,128)(2,1)}), bf16[2,4,256,1024]{3,1,0,2:T(4,128)(2,1)}, u32[]{:S(2)}, u32[]{:S(2)}) async-start(bf16[2,4,256,1024]{3,1,0,2:T(4,128)(2,1)} %copy.63), calls=%async_computation.2 | async-start | bytes 8388608 | tf_op jit(solution)/shard_map/all_to_all | solution.py:53
  17.5 7.4 %copy.62 = bf16[2,4,256,1024]{3,1,0,2:T(4,128)(2,1)} copy(bf16[2,4,256,1024]{3,2,1,0:T(8,128)(2,1)} %get-tuple-element.8) | data formatting | bytes 8388608
  24.8 86.1 %all-to-all-done.2 = bf16[2,4,256,1024]{3,1,0,2:T(4,128)(2,1)} async-done(((bf16[2,4,256,1024]{3,1,0,2:T(4,128)(2,1)}), bf16[2,4,256,1024]{3,1,0,2:T(4,128)(2,1)}, u32[]{:S(2)}, u32[]{:S(2)}) %all-to-all-start.2) | async-done | bytes 4194336 | tf_op jit(solution)/shard_map/all_to_all | solution.py:53
  110.9 5.1 %all-to-all-start = ((bf16[2,4,256,1024]{3,1,0,2:T(4,128)(2,1)}), bf16[2,4,256,1024]{3,1,0,2:T(4,128)(2,1)}, u32[]{:S(2)}, u32[]{:S(2)}) async-start(bf16[2,4,256,1024]{3,1,0,2:T(4,128)(2,1)} %copy.62), calls=%async_computation | async-start | bytes 8388608 | tf_op jit(solution)/shard_map/all_to_all | solution.py:53
  116.1 7.4 %copy.80 = bf16[2,4,4,64,1024]{4,2,3,1,0:T(4,128)(2,1)} copy(bf16[2,4,4,64,1024]{4,1,0,3,2:T(4,128)(2,1)} %bitcast.19) | data formatting | bytes 8388608 | tf_op jit(solution)/shard_map/all_to_all | solution.py:53
  123.4 12.0 %reshape.69 = bf16[2,256,64,64]{3,2,1,0:T(8,128)(2,1)} reshape(bf16[2,4,64,4,1024]{4,3,2,1,0:T(4,128)(2,1)} %bitcast.100) | data formatting | bytes 8388608 | tf_op jit(solution)/shard_map/reshape | solution.py:63
  135.5 13.9 %copy.38 = bf16[2,256,64,64]{1,2,0,3:T(8,128)(2,1)} copy(bf16[2,256,64,64]{3,2,1,0:T(8,128)(2,1)} %reshape.69) | data formatting | bytes 8388608 | tf_op jit(solution)/shard_map/reshape | solution.py:63
  149.4 3.6 fusion.10
  153.0 2.9 fusion.11
  155.9 6.4 %copy.40 = bf16[64,64,2,256]{3,2,1,0:T(2,128)(2,1)} copy(bf16[64,64,2,256]{3,1,2,0:T(8,128)(2,1)S(1)} %fusion.11) | data formatting | bytes 8388608 | tf_op jit(solution)/shard_map/convert_element_type | solution.py:67
  162.3 4.9 %copy.65 = bf16[512,8,2,256]{3,1,2,0:T(8,128)(2,1)} copy(bf16[512,8,2,256]{3,2,1,0:T(2,128)(2,1)} %bitcast.103) | data formatting | bytes 8388608
  167.2 20.2 %gather_fusion.2 = bf16[4096,512]{1,0:T(8,128)(2,1)} fusion(bf16[4096,512]{1,0:T(8,128)(2,1)} %bitcast.98, s32[4096]{0:T(1024)S(1)} %fusion.45), kind=kCustom, calls=%fused_computation.2 | custom fusion | bytes 8404992 | tf_op jit(solution)/shard_map/jit(_take)/gather | solution.py:68
  187.4 6.4 %copy.41 = bf16[32,128,512]{1,2,0:T(8,128)(2,1)} copy(bf16[32,128,512]{2,1,0:T(8,128)(2,1)} %bitcast.101) | data formatting | bytes 8388608 | tf_op jit(solution)/shard_map/reshape | solution.py:69
  193.9 14.8 %all-to-all-done = bf16[2,4,256,1024]{3,1,0,2:T(4,128)(2,1)} async-done(((bf16[2,4,256,1024]{3,1,0,2:T(4,128)(2,1)}), bf16[2,4,256,1024]{3,1,0,2:T(4,128)(2,1)}, u32[]{:S(2)}, u32[]{:S(2)}) %all-to-all-start) | async-done | bytes 4194336 | tf_op jit(solution)/shard_map/all_to_all | solution.py:53
  208.7 15.7 %all-to-all-start.3 = ((bf16[32,128,512]{1,2,0:T(8,128)(2,1)}), bf16[32,128,512]{1,2,0:T(8,128)(2,1)}, u32[]{:S(2)}, u32[]{:S(2)}) async-start(bf16[32,128,512]{1,2,0:T(8,128)(2,1)} %copy.41), calls=%async_computation.3 | async-start | bytes 8388608 | tf_op jit(solution)/shard_map/all_to_all | solution.py:73
  224.3 7.4 %copy.81 = bf16[2,4,4,64,1024]{4,2,3,1,0:T(4,128)(2,1)} copy(bf16[2,4,4,64,1024]{4,1,0,3,2:T(4,128)(2,1)} %bitcast.2) | data formatting | bytes 8388608 | tf_op jit(solution)/shard_map/all_to_all | solution.py:53
  231.7 12.0 %reshape.64 = bf16[2,256,64,64]{3,2,1,0:T(8,128)(2,1)} reshape(bf16[2,4,64,4,1024]{4,3,2,1,0:T(4,128)(2,1)} %bitcast.102) | data formatting | bytes 8388608 | tf_op jit(solution)/shard_map/reshape | solution.py:63
  243.8 13.6 %copy.30 = bf16[2,256,64,64]{1,2,0,3:T(8,128)(2,1)} copy(bf16[2,256,64,64]{3,2,1,0:T(8,128)(2,1)} %reshape.64) | data formatting | bytes 8388608 | tf_op jit(solution)/shard_map/reshape | solution.py:63
  257.3 3.6 fusion.8
  261.0 2.9 fusion.9
  263.9 6.4 %copy.32 = bf16[64,64,2,256]{3,2,1,0:T(2,128)(2,1)} copy(bf16[64,64,2,256]{3,1,2,0:T(8,128)(2,1)S(1)} %fusion.9) | data formatting | bytes 8388608 | tf_op jit(solution)/shard_map/convert_element_type | solution.py:67
  270.3 4.9 %copy.64 = bf16[512,8,2,256]{3,1,2,0:T(8,128)(2,1)} copy(bf16[512,8,2,256]{3,2,1,0:T(2,128)(2,1)} %bitcast.104) | data formatting | bytes 8388608
  275.1 20.2 %gather_fusion = bf16[4096,512]{1,0:T(8,128)(2,1)} fusion(bf16[4096,512]{1,0:T(8,128)(2,1)} %bitcast.97, s32[4096]{0:T(1024)S(1)} %fusion.45), kind=kCustom, calls=%fused_computation | custom fusion | bytes 8404992 | tf_op jit(solution)/shard_map/jit(_take)/gather | solution.py:68
  295.4 6.4 %copy.33 = bf16[32,128,512]{1,2,0:T(8,128)(2,1)} copy(bf16[32,128,512]{2,1,0:T(8,128)(2,1)} %bitcast.99) | data formatting | bytes 8388608 | tf_op jit(solution)/shard_map/reshape | solution.py:69
  301.8 16.4 %all-to-all-done.3 = bf16[32,128,512]{1,2,0:T(8,128)(2,1)} async-done(((bf16[32,128,512]{1,2,0:T(8,128)(2,1)}), bf16[32,128,512]{1,2,0:T(8,128)(2,1)}, u32[]{:S(2)}, u32[]{:S(2)}) %all-to-all-start.3) | async-done | bytes 4194336 | tf_op jit(solution)/shard_map/all_to_all | solution.py:73
  318.2 4.0 all-to-all-start.1
  322.3 0.6 copy.45
  323.0 1.1 gather_fusion.1
  324.1 0.6 gather_fusion.3
  325.1 5.5 %copy.42 = bf16[128,2,4,8,4,64]{0,5,4,3,2,1:T(8,128)(2,1)} copy(bf16[128,2,4,8,4,64]{0,5,2,1,3,4:T(8,128)(2,1)} %bitcast.31) | data formatting | bytes 8388608 | tf_op jit(solution)/shard_map/transpose | solution.py:78
  330.6 7.9 %copy.43 = bf16[128,2,4,2048]{3,2,1,0:T(4,128)(2,1)} copy(bf16[128,2,4,2048]{0,3,2,1:T(8,128)(2,1)} %bitcast.105) | data formatting | bytes 8388608 | tf_op jit(solution)/shard_map/reshape | solution.py:79
  338.5 77.6 %all-to-all-done.1 = bf16[32,128,512]{1,2,0:T(8,128)(2,1)} async-done(((bf16[32,128,512]{1,2,0:T(8,128)(2,1)}), bf16[32,128,512]{1,2,0:T(8,128)(2,1)}, u32[]{:S(2)}, u32[]{:S(2)}) %all-to-all-start.1) | async-done | bytes 4194336 | tf_op jit(solution)/shard_map/all_to_all | solution.py:73
  416.2 5.5 %copy.34 = bf16[128,2,4,8,4,64]{0,5,4,3,2,1:T(8,128)(2,1)} copy(bf16[128,2,4,8,4,64]{0,5,2,1,3,4:T(8,128)(2,1)} %bitcast.14) | data formatting | bytes 8388608 | tf_op jit(solution)/shard_map/transpose | solution.py:78
  421.7 7.9 %copy.35 = bf16[128,2,4,2048]{3,2,1,0:T(4,128)(2,1)} copy(bf16[128,2,4,2048]{0,3,2,1:T(8,128)(2,1)} %bitcast.106) | data formatting | bytes 8388608 | tf_op jit(solution)/shard_map/reshape | solution.py:79
  429.6 16.7 %fusion = f32[128,2,4,64]{3,2,1,0:T(4,128)S(1)} fusion(bf16[128,2,4,2048]{3,2,1,0:T(4,128)(2,1)} %copy.43, bf16[128,64,2048]{2,1,0:T(8,128)(2,1)} %param.10, pred[128,2048]{1,0:T(8,128)(4,1)S(1)} %iota_compare_fusion), kind=kOutput, calls=%fused_computation.4 | convolution fusion | flops 285212672 | bytes 38273024 | tf_op jit(solution)/shard_map/sxcb,skb->sxck/dot_general | solution.py:80
  446.3 16.9 %fusion.2 = f32[128,2,4,64]{3,2,1,0:T(4,128)S(1)} fusion(bf16[128,2,4,2048]{3,2,1,0:T(4,128)(2,1)} %copy.35, bf16[128,64,2048]{2,1,0:T(8,128)(2,1)} %param.10, pred[128,2048]{1,0:T(8,128)(4,1)S(1)} %iota_compare_fusion), kind=kOutput, calls=%fused_computation.6 | convolution fusion | flops 285212672 | bytes 38273024 | tf_op jit(solution)/shard_map/sxcb,skb->sxck/dot_general | solution.py:80
  463.3 0.3 fusion.38
  463.9 4.2 fusion.32
  468.1 0.7 reshape.122
  468.8 3.9 all-to-all-start.4
  472.7 0.3 fusion.35
  473.1 1.1 copy.48
  474.2 5.8 %all-to-all-done.4 = f32[32,1,256]{2,1,0:T(1,128)S(1)} async-done(((f32[32,1,256]{2,1,0:T(1,128)}), f32[32,1,256]{2,1,0:T(1,128)S(1)}, u32[]{:S(2)}, u32[]{:S(2)}) %all-to-all-start.4) | async-done | bytes 32800 | tf_op jit(solution)/shard_map/all_to_all | solution.py:93
  480.0 0.5 broadcast.62
  480.5 0.7 reduce
  481.4 0.6 broadcast_multiply_fusion
  (22 shorter events, 0.8 us)
Async XLA Ops:
  0.6 322.3 %copy-start = (s32[4096]{0:T(1024)S(1)}, s32[4096]{0:T(1024)}, u32[]{:S(2)}) copy-start(s32[4096]{0:T(1024)} %param.11) | copy-start | bytes 49156
  11.1 99.7 %all-to-all-start.2 = ((bf16[2,4,256,1024]{3,1,0,2:T(4,128)(2,1)}), bf16[2,4,256,1024]{3,1,0,2:T(4,128)(2,1)}, u32[]{:S(2)}, u32[]{:S(2)}) async-start(bf16[2,4,256,1024]{3,1,0,2:T(4,128)(2,1)} %copy.63), calls=%async_computation.2 | async-start | bytes 8388608 | tf_op jit(solution)/shard_map/all_to_all | solution.py:53
  24.8 91.2 %copy-start.5 = (s32[4096]{0:T(1024)S(1)}, s32[4096]{0:T(1024)}, u32[]{:S(2)}) copy-start(s32[4096]{0:T(1024)} %param.12) | copy-start | bytes 49156
  110.9 97.8 %all-to-all-start = ((bf16[2,4,256,1024]{3,1,0,2:T(4,128)(2,1)}), bf16[2,4,256,1024]{3,1,0,2:T(4,128)(2,1)}, u32[]{:S(2)}, u32[]{:S(2)}) async-start(bf16[2,4,256,1024]{3,1,0,2:T(4,128)(2,1)} %copy.62), calls=%async_computation | async-start | bytes 8388608 | tf_op jit(solution)/shard_map/all_to_all | solution.py:53
  135.5 13.9 %copy-start.3 = (bf16[2,2,64,64,1]{3,2,1,4,0:T(8,128)(2,1)S(1)}, bf16[2,2,64,64,1]{3,2,1,4,0:T(8,128)(2,1)}, u32[]{:S(2)}) copy-start(bf16[2,2,64,64,1]{3,2,1,4,0:T(8,128)(2,1)} %constant.62) | copy-start | bytes 98308
  149.4 3.7 copy-start.1
  208.7 109.6 %all-to-all-start.3 = ((bf16[32,128,512]{1,2,0:T(8,128)(2,1)}), bf16[32,128,512]{1,2,0:T(8,128)(2,1)}, u32[]{:S(2)}, u32[]{:S(2)}) async-start(bf16[32,128,512]{1,2,0:T(8,128)(2,1)} %copy.41), calls=%async_computation.3 | async-start | bytes 8388608 | tf_op jit(solution)/shard_map/all_to_all | solution.py:73
  257.3 3.6 copy-start.2
  301.8 20.5 %copy-start.4 = (s32[4096,8]{0,1:T(8,128)S(1)}, s32[4096,8]{0,1:T(8,128)}, u32[]{:S(2)}) copy-start(s32[4096,8]{0,1:T(8,128)} %param.13) | copy-start | bytes 393220
  318.2 98.0 %all-to-all-start.1 = ((bf16[32,128,512]{1,2,0:T(8,128)(2,1)}), bf16[32,128,512]{1,2,0:T(8,128)(2,1)}, u32[]{:S(2)}, u32[]{:S(2)}) async-start(bf16[32,128,512]{1,2,0:T(8,128)(2,1)} %copy.33), calls=%async_computation.1 | async-start | bytes 8388608 | tf_op jit(solution)/shard_map/all_to_all | solution.py:73
  468.8 11.2 %all-to-all-start.4 = ((f32[32,1,256]{2,1,0:T(1,128)}), f32[32,1,256]{2,1,0:T(1,128)S(1)}, u32[]{:S(2)}, u32[]{:S(2)}) async-start(f32[32,1,256]{2,1,0:T(1,128)} %reshape.122), calls=%async_computation.4 | async-start | bytes 65536 | tf_op jit(solution)/shard_map/all_to_all | solution.py:93

commit v3 on v2

--- a/solution.py
+++ b/solution.py
@@ -79,7 +79,12 @@
         owned = owned.reshape(slots, 2, part, baselines)
         return jnp.einsum("sxcb,skb->sxck", owned, masked, preferred_element_type=jnp.float32)
 
-    coeffs = jnp.concatenate([filtered(one) for one in moved], axis=2)
+    pieces = []
+    for one in moved:
+        if pieces:
+            one, pieces[-1] = lax.optimization_barrier((one, pieces[-1]))
+        pieces.append(filtered(one))
+    coeffs = jnp.concatenate(pieces, axis=2)
     kl_coeffs = coeffs.astype(jnp.bfloat16)
     power = coeffs[:, 0] * coeffs[:, 0] + coeffs[:, 1] * coeffs[:, 1]
     block_power = power.reshape(slots, channels, blocks, modes_kept // blocks).sum(axis=-1)

time: 490 us -> 474 us (0.967)
  waiting for transfers between devices: 201 us -> 184 us
    all_to_all x2, waiting for transfers between devices: 94.1 us -> 77.3 us  [body(): lax.all_to_all(one, ('grp', 'wide'), split_axis=0, concat_axis=0, tiled=T...]
  transfers between devices with their start and end apart: 5 -> 5, of which waited for: 5 -> 5; matrix products, arithmetic and copies ran while one was open for 37% -> 42% of each run, Pallas kernels for 0% -> 0%
where the time goes in v3:
time: 474 us; the launch traced here: 466 us
  local copies, waits for them, and re-layouts  192 us (41%)
  waiting for transfers between devices  184 us (39%)
  matrix products  50.8 us (11%)
  starting transfers between devices  35.1 us (7%)
    all_to_all x2, waiting for transfers between devices, body(): lax.all_to_all(lax.slice_in_dim(visibilities, i * part, (i + 1) * part, a...  101 us
    all_to_all x2, waiting for transfers between devices, body(): lax.all_to_all(one, ('grp', 'wide'), split_axis=0, concat_axis=0, tiled=T...  77.3 us
    reshape x4, local copies, waits for them, and re-layouts, transform(): samples = local.reshape(2, rows, n1, n2)  51.5 us
    gather x2, local copies, waits for them, and re-layouts, transform(): ordered = jnp.take(spectrum, place_of_slot, axis=0, mode='clip')  40.5 us
    dot_general x2, matrix products, filtered(): jnp.einsum('sxcb,skb->sxck', owned, masked, preferred_element_type=jnp.fl...  33.6 us
    unnamed x20, local copies, waits for them, and re-layouts  24.9 us
    all_to_all x2, starting transfers between devices, body(): lax.all_to_all(one, ('grp', 'wide'), split_axis=0, concat_axis=0, tiled=T...  19.7 us
    reshape x2, local copies, waits for them, and re-layouts, filtered(): owned = owned.reshape(slots, 2, part, baselines)  15.9 us
  transfers between devices with their start and end apart: 5, of which 5 were waited for; matrix products, arithmetic and copies ran while one was open for 42% of the time, Pallas kernels for 0%

profile of v3, /device:TPU:0, one launch (start us, length us, event | category | flops | bytes accessed | tf_op | source)
XLA Modules:
  0.0 465.7 jit_solution(2942067508688501458)
XLA Ops:
  0.6 5.3 %fusion.52 = (bf16[2,4,256,1024]{3,2,1,0:T(8,128)(2,1)S(1)}, bf16[2,4,256,1024]{3,2,1,0:T(8,128)(2,1)}) fusion(bf16[2,8,256,1024]{3,2,1,0:T(8,128)(2,1)} %param.9), kind=kLoop, calls=%fused_computation.70 | loop fusion | bytes 16777216 | tf_op jit(solution)/shard_map/slice | solution.py:54
  6.0 5.2 %copy.64 = bf16[2,4,256,1024]{3,1,0,2:T(4,128)(2,1)} copy(bf16[2,4,256,1024]{3,2,1,0:T(8,128)(2,1)S(1)} %get-tuple-element.12) | data formatting | bytes 8388608
  11.2 6.3 %all-to-all-start.2 = ((bf16[2,4,256,1024]{3,1,0,2:T(4,128)(2,1)}), bf16[2,4,256,1024]{3,1,0,2:T(4,128)(2,1)}, u32[]{:S(2)}, u32[]{:S(2)}) async-start(bf16[2,4,256,1024]{3,1,0,2:T(4,128)(2,1)} %copy.64), calls=%async_computation.2 | async-start | bytes 8388608 | tf_op jit(solution)/shard_map/all_to_all | solution.py:53
  17.5 7.4 %copy.63 = bf16[2,4,256,1024]{3,1,0,2:T(4,128)(2,1)} copy(bf16[2,4,256,1024]{3,2,1,0:T(8,128)(2,1)} %get-tuple-element.13) | data formatting | bytes 8388608
  24.8 86.1 %all-to-all-done.2 = bf16[2,4,256,1024]{3,1,0,2:T(4,128)(2,1)} async-done(((bf16[2,4,256,1024]{3,1,0,2:T(4,128)(2,1)}), bf16[2,4,256,1024]{3,1,0,2:T(4,128)(2,1)}, u32[]{:S(2)}, u32[]{:S(2)}) %all-to-all-start.2) | async-done | bytes 4194336 | tf_op jit(solution)/shard_map/all_to_all | solution.py:53
  110.9 5.1 %all-to-all-start = ((bf16[2,4,256,1024]{3,1,0,2:T(4,128)(2,1)}), bf16[2,4,256,1024]{3,1,0,2:T(4,128)(2,1)}, u32[]{:S(2)}, u32[]{:S(2)}) async-start(bf16[2,4,256,1024]{3,1,0,2:T(4,128)(2,1)} %copy.63), calls=%async_computation | async-start | bytes 8388608 | tf_op jit(solution)/shard_map/all_to_all | solution.py:53
  116.1 7.4 %copy.81 = bf16[2,4,4,64,1024]{4,2,3,1,0:T(4,128)(2,1)} copy(bf16[2,4,4,64,1024]{4,1,0,3,2:T(4,128)(2,1)} %bitcast.14) | data formatting | bytes 8388608 | tf_op jit(solution)/shard_map/all_to_all | solution.py:53
  123.5 12.0 %reshape.67 = bf16[2,256,64,64]{3,2,1,0:T(8,128)(2,1)} reshape(bf16[2,4,64,4,1024]{4,3,2,1,0:T(4,128)(2,1)} %bitcast.100) | data formatting | bytes 8388608 | tf_op jit(solution)/shard_map/reshape | solution.py:63
  135.5 13.9 %copy.37 = bf16[2,256,64,64]{1,2,0,3:T(8,128)(2,1)} copy(bf16[2,256,64,64]{3,2,1,0:T(8,128)(2,1)} %reshape.67) | data formatting | bytes 8388608 | tf_op jit(solution)/shard_map/reshape | solution.py:63
  149.4 3.6 fusion.10
  153.0 2.9 fusion.11
  155.9 6.4 %copy.39 = bf16[64,64,2,256]{3,2,1,0:T(2,128)(2,1)} copy(bf16[64,64,2,256]{3,1,2,0:T(8,128)(2,1)S(1)} %fusion.11) | data formatting | bytes 8388608 | tf_op jit(solution)/shard_map/convert_element_type | solution.py:67
  162.3 4.9 %copy.66 = bf16[512,8,2,256]{3,1,2,0:T(8,128)(2,1)} copy(bf16[512,8,2,256]{3,2,1,0:T(2,128)(2,1)} %bitcast.103) | data formatting | bytes 8388608
  167.2 20.2 %gather_fusion.1 = bf16[4096,512]{1,0:T(8,128)(2,1)} fusion(bf16[4096,512]{1,0:T(8,128)(2,1)} %bitcast.98, s32[4096]{0:T(1024)S(1)} %fusion.45), kind=kCustom, calls=%fused_computation.1 | custom fusion | bytes 8404992 | tf_op jit(solution)/shard_map/jit(_take)/gather | solution.py:68
  187.4 6.4 %copy.40 = bf16[32,128,512]{1,2,0:T(8,128)(2,1)} copy(bf16[32,128,512]{2,1,0:T(8,128)(2,1)} %bitcast.101) | data formatting | bytes 8388608 | tf_op jit(solution)/shard_map/reshape | solution.py:69
  193.9 14.8 %all-to-all-done = bf16[2,4,256,1024]{3,1,0,2:T(4,128)(2,1)} async-done(((bf16[2,4,256,1024]{3,1,0,2:T(4,128)(2,1)}), bf16[2,4,256,1024]{3,1,0,2:T(4,128)(2,1)}, u32[]{:S(2)}, u32[]{:S(2)}) %all-to-all-start) | async-done | bytes 4194336 | tf_op jit(solution)/shard_map/all_to_all | solution.py:53
  208.7 15.7 %all-to-all-start.3 = ((bf16[32,128,512]{1,2,0:T(8,128)(2,1)}), bf16[32,128,512]{1,2,0:T(8,128)(2,1)}, u32[]{:S(2)}, u32[]{:S(2)}) async-start(bf16[32,128,512]{1,2,0:T(8,128)(2,1)} %copy.40), calls=%async_computation.3 | async-start | bytes 8388608 | tf_op jit(solution)/shard_map/all_to_all | solution.py:73
  224.4 7.4 %copy.82 = bf16[2,4,4,64,1024]{4,2,3,1,0:T(4,128)(2,1)} copy(bf16[2,4,4,64,1024]{4,1,0,3,2:T(4,128)(2,1)} %bitcast.2) | data formatting | bytes 8388608 | tf_op jit(solution)/shard_map/all_to_all | solution.py:53
  231.8 12.0 %reshape.64 = bf16[2,256,64,64]{3,2,1,0:T(8,128)(2,1)} reshape(bf16[2,4,64,4,1024]{4,3,2,1,0:T(4,128)(2,1)} %bitcast.102) | data formatting | bytes 8388608 | tf_op jit(solution)/shard_map/reshape | solution.py:63
  243.8 13.6 %copy.31 = bf16[2,256,64,64]{1,2,0,3:T(8,128)(2,1)} copy(bf16[2,256,64,64]{3,2,1,0:T(8,128)(2,1)} %reshape.64) | data formatting | bytes 8388608 | tf_op jit(solution)/shard_map/reshape | solution.py:63
  257.3 3.6 fusion.8
  261.0 2.9 fusion.9
  263.9 6.4 %copy.33 = bf16[64,64,2,256]{3,2,1,0:T(2,128)(2,1)} copy(bf16[64,64,2,256]{3,1,2,0:T(8,128)(2,1)S(1)} %fusion.9) | data formatting | bytes 8388608 | tf_op jit(solution)/shard_map/convert_element_type | solution.py:67
  270.3 4.9 %copy.65 = bf16[512,8,2,256]{3,1,2,0:T(8,128)(2,1)} copy(bf16[512,8,2,256]{3,2,1,0:T(2,128)(2,1)} %bitcast.104) | data formatting | bytes 8388608
  275.1 20.2 %gather_fusion = bf16[4096,512]{1,0:T(8,128)(2,1)} fusion(bf16[4096,512]{1,0:T(8,128)(2,1)} %bitcast.97, s32[4096]{0:T(1024)S(1)} %fusion.45), kind=kCustom, calls=%fused_computation | custom fusion | bytes 8404992 | tf_op jit(solution)/shard_map/jit(_take)/gather | solution.py:68
  295.4 6.4 %copy.34 = bf16[32,128,512]{1,2,0:T(8,128)(2,1)} copy(bf16[32,128,512]{2,1,0:T(8,128)(2,1)} %bitcast.99) | data formatting | bytes 8388608 | tf_op jit(solution)/shard_map/reshape | solution.py:69
  301.8 16.4 %all-to-all-done.3 = bf16[32,128,512]{1,2,0:T(8,128)(2,1)} async-done(((bf16[32,128,512]{1,2,0:T(8,128)(2,1)}), bf16[32,128,512]{1,2,0:T(8,128)(2,1)}, u32[]{:S(2)}, u32[]{:S(2)}) %all-to-all-start.3) | async-done | bytes 4194336 | tf_op jit(solution)/shard_map/all_to_all | solution.py:73
  318.2 4.0 all-to-all-start.1
  322.3 0.6 copy.46
  323.0 1.1 gather_fusion.2
  324.1 0.6 gather_fusion.3
  325.1 5.5 %copy.41 = bf16[128,2,4,8,4,64]{0,5,4,3,2,1:T(8,128)(2,1)} copy(bf16[128,2,4,8,4,64]{0,5,2,1,3,4:T(8,128)(2,1)} %bitcast.26) | data formatting | bytes 8388608 | tf_op jit(solution)/shard_map/transpose | solution.py:78
  330.6 8.0 %copy.42 = bf16[128,2,4,2048]{3,2,1,0:T(4,128)(2,1)} copy(bf16[128,2,4,2048]{0,3,2,1:T(8,128)(2,1)} %bitcast.105) | data formatting | bytes 8388608 | tf_op jit(solution)/shard_map/reshape | solution.py:79
  338.6 16.7 %fusion.2 = f32[128,2,4,64]{3,2,1,0:T(4,128)S(1)} fusion(bf16[128,2,4,2048]{3,2,1,0:T(4,128)(2,1)} %copy.42, bf16[128,64,2048]{2,1,0:T(8,128)(2,1)} %param.10, pred[128,2048]{1,0:T(8,128)(4,1)S(1)} %iota_compare_fusion), kind=kOutput, calls=%fused_computation.6 | convolution fusion | flops 285212672 | bytes 38273024 | tf_op jit(solution)/shard_map/sxcb,skb->sxck/dot_general | solution.py:80
  355.3 60.9 %all-to-all-done.1 = bf16[32,128,512]{1,2,0:T(8,128)(2,1)} async-done(((bf16[32,128,512]{1,2,0:T(8,128)(2,1)}), bf16[32,128,512]{1,2,0:T(8,128)(2,1)}, u32[]{:S(2)}, u32[]{:S(2)}) %all-to-all-start.1) | async-done | bytes 4194336 | tf_op jit(solution)/shard_map/all_to_all | solution.py:73
  416.2 5.5 %copy.43 = bf16[128,2,4,8,4,64]{0,5,4,3,2,1:T(8,128)(2,1)} copy(bf16[128,2,4,8,4,64]{0,5,2,1,3,4:T(8,128)(2,1)} %bitcast.31) | data formatting | bytes 8388608 | tf_op jit(solution)/shard_map/transpose | solution.py:78
  421.7 7.9 %copy.44 = bf16[128,2,4,2048]{3,2,1,0:T(4,128)(2,1)} copy(bf16[128,2,4,2048]{0,3,2,1:T(8,128)(2,1)} %bitcast.106) | data formatting | bytes 8388608 | tf_op jit(solution)/shard_map/reshape | solution.py:79
  429.7 16.9 %fusion = f32[128,2,4,64]{3,2,1,0:T(4,128)S(1)} fusion(bf16[128,2,4,2048]{3,2,1,0:T(4,128)(2,1)} %copy.44, bf16[128,64,2048]{2,1,0:T(8,128)(2,1)} %param.10, pred[128,2048]{1,0:T(8,128)(4,1)S(1)} %iota_compare_fusion), kind=kOutput, calls=%fused_computation.4 | convolution fusion | flops 285212672 | bytes 38273024 | tf_op jit(solution)/shard_map/sxcb,skb->sxck/dot_general | solution.py:80
  446.6 0.3 fusion.38
  447.2 4.2 fusion.32
  451.4 0.7 reshape.122
  452.1 3.9 all-to-all-start.4
  456.1 0.3 fusion.35
  456.4 1.1 copy.49
  457.5 5.8 %all-to-all-done.4 = f32[32,1,256]{2,1,0:T(1,128)S(1)} async-done(((f32[32,1,256]{2,1,0:T(1,128)}), f32[32,1,256]{2,1,0:T(1,128)S(1)}, u32[]{:S(2)}, u32[]{:S(2)}) %all-to-all-start.4) | async-done | bytes 32800 | tf_op jit(solution)/shard_map/all_to_all | solution.py:98
  463.3 0.5 broadcast.62
  463.8 0.7 reduce
  464.7 0.6 broadcast_multiply_fusion
  (22 shorter events, 0.8 us)
Async XLA Ops:
  0.6 322.4 %copy-start = (s32[4096]{0:T(1024)S(1)}, s32[4096]{0:T(1024)}, u32[]{:S(2)}) copy-start(s32[4096]{0:T(1024)} %param.11) | copy-start | bytes 49156
  11.2 99.7 %all-to-all-start.2 = ((bf16[2,4,256,1024]{3,1,0,2:T(4,128)(2,1)}), bf16[2,4,256,1024]{3,1,0,2:T(4,128)(2,1)}, u32[]{:S(2)}, u32[]{:S(2)}) async-start(bf16[2,4,256,1024]{3,1,0,2:T(4,128)(2,1)} %copy.64), calls=%async_computation.2 | async-start | bytes 8388608 | tf_op jit(solution)/shard_map/all_to_all | solution.py:53
  24.8 91.2 %copy-start.5 = (s32[4096]{0:T(1024)S(1)}, s32[4096]{0:T(1024)}, u32[]{:S(2)}) copy-start(s32[4096]{0:T(1024)} %param.12) | copy-start | bytes 49156
  110.9 97.8 %all-to-all-start = ((bf16[2,4,256,1024]{3,1,0,2:T(4,128)(2,1)}), bf16[2,4,256,1024]{3,1,0,2:T(4,128)(2,1)}, u32[]{:S(2)}, u32[]{:S(2)}) async-start(bf16[2,4,256,1024]{3,1,0,2:T(4,128)(2,1)} %copy.63), calls=%async_computation | async-start | bytes 8388608 | tf_op jit(solution)/shard_map/all_to_all | solution.py:53
  135.5 13.9 %copy-start.3 = (bf16[2,2,64,64,1]{3,2,1,4,0:T(8,128)(2,1)S(1)}, bf16[2,2,64,64,1]{3,2,1,4,0:T(8,128)(2,1)}, u32[]{:S(2)}) copy-start(bf16[2,2,64,64,1]{3,2,1,4,0:T(8,128)(2,1)} %constant.62) | copy-start | bytes 98308
  149.4 3.6 copy-start.1
  208.7 109.6 %all-to-all-start.3 = ((bf16[32,128,512]{1,2,0:T(8,128)(2,1)}), bf16[32,128,512]{1,2,0:T(8,128)(2,1)}, u32[]{:S(2)}, u32[]{:S(2)}) async-start(bf16[32,128,512]{1,2,0:T(8,128)(2,1)} %copy.40), calls=%async_computation.3 | async-start | bytes 8388608 | tf_op jit(solution)/shard_map/all_to_all | solution.py:73
  257.3 3.6 copy-start.2
  301.8 20.5 %copy-start.4 = (s32[4096,8]{0,1:T(8,128)S(1)}, s32[4096,8]{0,1:T(8,128)}, u32[]{:S(2)}) copy-start(s32[4096,8]{0,1:T(8,128)} %param.13) | copy-start | bytes 393220
  318.2 98.0 %all-to-all-start.1 = ((bf16[32,128,512]{1,2,0:T(8,128)(2,1)}), bf16[32,128,512]{1,2,0:T(8,128)(2,1)}, u32[]{:S(2)}, u32[]{:S(2)}) async-start(bf16[32,128,512]{1,2,0:T(8,128)(2,1)} %copy.34), calls=%async_computation.1 | async-start | bytes 8388608 | tf_op jit(solution)/shard_map/all_to_all | solution.py:73
  452.1 11.2 %all-to-all-start.4 = ((f32[32,1,256]{2,1,0:T(1,128)}), f32[32,1,256]{2,1,0:T(1,128)S(1)}, u32[]{:S(2)}, u32[]{:S(2)}) async-start(f32[32,1,256]{2,1,0:T(1,128)} %reshape.122), calls=%async_computation.4 | async-start | bytes 65536 | tf_op jit(solution)/shard_map/all_to_all | solution.py:98
